TPU v7x, 32 devices: a whole 2x2x4 slice. The times are simulated.
32 devices in a mesh: scen: 2 (over y), region: 4 (over z), dest: 4 (over x, core).
Axes of the slice: x: 2, y: 2, z: 4, core: 2. Of those that a mesh axis runs over, the one named last changes fastest.
Arguments:
- density: float32 [8, 1024, 1024], P(None, ('scen', 'region'), 'dest'), parts along dimension 1, may hold values from 0.01 to 1.5, as said below
- anchor: float32 [1024, 1024], P(('scen', 'region'), 'dest'), parts along dimension 0, may hold values from 0.005 to 0.3
- feeds: int32 [512, 4], P('region'), may hold values from -1 to 511, as said below
- turns: int32 [512, 4], P('region'), may hold values from 1 to 8
- plan: int32 [3, 512], P(None, 'region'), may hold values from 0 to 7
- capacity_levels: float32 [8], replicated, may hold values from 0.2 to 0.8
Outputs:
- final_density: float32 [8, 1024, 1024], P(None, ('scen', 'region'), 'dest'), parts along dimension 1
There are 2 independent parts, one for each index of `scen`. A program takes and returns all parts, laid end to end along the dimension named above; an argument that names none is the same for every part. Nothing has to cross between parts.
Inputs may be any that keep to these rules, and one draw needn't show every extreme that they name: Each per-commodity density is positive. `feeds`: -1 marks an unused entry. The lists of one device's links hold at most 64 entries naming links of any one other device, and name at most 32 distinct links of it; every device reaches both bounds for some other device.
All inputs are finite; a program needn't handle non-finite values.
Results may differ from a plain program's by a relative error of at most 0.0001.
Values sent between devices are 32-bit elements; how exact they have to be, the bound alone decides.
A program may use at most 64 MiB of HBM per device.

v0:
```python
import jax
import jax.numpy as jnp
from jax import lax
from jax.sharding import PartitionSpec as P

COMM = 1024


FREE_SPEED = 0.8
WAVE_SPEED = 0.4
JAM_FACTOR = 2.0
EXIT_WEIGHT = 4.0


def one_hot_table(positions, segments):
    return positions[:, None] == jnp.arange(segments, dtype=jnp.int32)[None, :]


def table_total(values, table):
    return jnp.sum(jnp.where(table, values[:, None], 0), axis=0)


def slot_ranks(chosen, owners, peers):
    member = chosen[:, None] & (owners[:, None] == jnp.arange(peers, dtype=jnp.int32)[None, :])
    ranked = jnp.cumsum(member.astype(jnp.int32), axis=0) - 1
    return jnp.sum(jnp.where(member, ranked, 0), axis=1)


def local(density, anchor, feeds, turns, plan, capacity_levels):
    num_cells, num_links, commodity_width = density.shape
    peers = lax.axis_size("region")
    my_region = lax.axis_index("region")
    bucket = 4 * max(1, (num_links // 2 + 4 * (peers - 2) - 1) // (4 * (peers - 2)))
    flat_feed = feeds.reshape(-1)
    flat_turn = turns.reshape(-1)
    is_live = flat_feed >= 0
    owners = jnp.where(is_live, flat_feed // num_links, -1)
    local_ids = jnp.where(is_live, flat_feed % num_links, 0)
    is_remote = is_live & (owners != my_region)
    is_nearby = is_live & (owners == my_region)
    capacity = 2 * bucket
    slots = slot_ranks(is_remote, owners, peers)
    total_slots = peers * capacity
    leader_flat = jnp.where(is_remote, owners * capacity + slots, -1)
    route_flat = jnp.where(is_remote, owners * capacity + slots, -1)
    leader_table = one_hot_table(leader_flat, total_slots)
    route_table = one_hot_table(route_flat, total_slots)
    id_filled = table_total(local_ids, leader_table)
    request_ids = jnp.where(jnp.any(leader_table, axis=0), id_filled, -1).reshape(peers, capacity)
    request_counts = table_total(flat_turn, route_table).reshape(peers, capacity)
    asked_ids, asked_counts = (
        lax.all_to_all(request_ids, "region", split_axis=0, concat_axis=0, tiled=True),
        lax.all_to_all(request_counts, "region", split_axis=0, concat_axis=0, tiled=True),
    )
    flat_asked = asked_ids.reshape(-1)
    nearby_rows = jnp.where(is_nearby, local_ids, -1)
    nearby_table = one_hot_table(nearby_rows, num_links)
    asked_table = one_hot_table(flat_asked, num_links)
    count_total = table_total(jnp.where(is_nearby, flat_turn, 0), nearby_table)
    count_total = count_total + table_total(asked_counts.reshape(-1), asked_table)
    denominator = count_total.astype(jnp.float32) + EXIT_WEIGHT
    gather_ids = jnp.maximum(flat_asked, 0)
    pick_peer = jnp.where(is_remote, owners, 0)
    pick_slot = jnp.where(is_remote, slots, 0)
    live_weight = jnp.where(is_live, flat_turn, 0).astype(jnp.float32)
    level_ids = jnp.arange(capacity_levels.shape[0], dtype=jnp.int32)
    cell_sum, anchor_total = lax.psum((jnp.sum(density, axis=2), jnp.sum(anchor, axis=1)), "dest")
    for step_index in range(plan.shape[0]):
        last_rows = density[num_cells - 1]
        if step_index > 0:
            cell_sum = lax.psum(jnp.sum(density, axis=2), "dest")
        level_match = plan[step_index][:, None] == level_ids[None, :]
        capacity_now = jnp.sum(jnp.where(level_match, capacity_levels[None, :], 0.0), axis=1) * COMM
        sending = jnp.minimum(FREE_SPEED * cell_sum, capacity_now[None, :])
        receiving = jnp.minimum(capacity_now[None, :], WAVE_SPEED * (JAM_FACTOR * COMM - cell_sum))
        per_count = sending[num_cells - 1] / denominator
        unit_share = per_count / cell_sum[num_cells - 1]
        sent_count = per_count[gather_ids].reshape(peers, capacity)
        sent_unit = unit_share[gather_ids].reshape(peers, capacity)
        sent_rows = last_rows[gather_ids].reshape(peers, capacity, commodity_width)
        got_rows, got_count, got_unit = (
            lax.all_to_all(sent_rows, "region", split_axis=0, concat_axis=0, tiled=True),
            lax.all_to_all(sent_count, "region", split_axis=0, concat_axis=0, tiled=True),
            lax.all_to_all(sent_unit, "region", split_axis=0, concat_axis=0, tiled=True),
        )
        pair_count = jnp.where(is_remote, got_count[pick_peer, pick_slot], per_count[local_ids])
        pair_unit = jnp.where(is_remote, got_unit[pick_peer, pick_slot], unit_share[local_ids])
        pair_rows = jnp.where(
            is_remote[:, None], got_rows[pick_peer, pick_slot], last_rows[local_ids]
        )
        demand = jnp.sum((live_weight * pair_count).reshape(num_links, 4), axis=1) + anchor_total
        ratio = receiving[0] / jnp.maximum(receiving[0], demand)
        mixing = (live_weight * pair_unit).reshape(num_links, 4)
        gathered = jnp.sum(
            mixing[:, :, None] * pair_rows.reshape(num_links, 4, commodity_width), axis=1
        )
        inflow = ratio[:, None] * (gathered + anchor)
        granted = (live_weight.reshape(num_links, 4) * ratio[:, None]).reshape(-1)
        send_back = table_total(granted, route_table).reshape(peers, capacity)
        returned = lax.all_to_all(send_back, "region", split_axis=0, concat_axis=0, tiled=True)
        passed = table_total(jnp.where(is_nearby, granted, 0.0), nearby_table)
        passed = passed + table_total(returned.reshape(-1), asked_table)
        outflow = (unit_share * (passed + EXIT_WEIGHT))[:, None] * last_rows
        through = jnp.minimum(sending[:-1], receiving[1:])
        moving = (through / cell_sum[:-1])[:, :, None] * density[:-1]
        density = (
            density
            - jnp.pad(moving, ((0, 1), (0, 0), (0, 0)))
            + jnp.pad(moving, ((1, 0), (0, 0), (0, 0)))
        )
        density = jnp.concatenate(
            [
                density[:1] + inflow[None],
                density[1 : num_cells - 1],
                density[num_cells - 1 :] - outflow[None],
            ],
            axis=0,
        )
    return density


def solution(mesh):
    in_specs = (
        P(None, ("scen", "region"), "dest"),
        P(("scen", "region"), "dest"),
        P("region", None),
        P("region", None),
        P(None, "region"),
        P(),
    )
    out_specs = P(None, ("scen", "region"), "dest")
    return jax.shard_map(local, mesh=mesh, in_specs=in_specs, out_specs=out_specs, check_vma=False)
```

profile of v0, /device:TPU:0, one launch (start us, length us, event | category | flops | bytes accessed | tf_op | source)
XLA Modules:
  0.0 228.3 jit_solution(14562001731284623854)
XLA Ops:
  1.1 1.2 reduce-window.6
  4.9 6.3 %all-to-all-start = ((s32[4,1,64]{2,1,0:T(1,128)}), s32[4,1,64]{2,1,0:T(1,128)S(1)}, u32[]{:S(2)}, u32[]{:S(2)}) async-start(s32[4,1,64]{2,1,0:T(1,128)} %select_n.421), calls=%async_computation | async-start | bytes 4096 | tf_op jit(solution)/shard_map/all_to_all | solution.py:52
  13.6 1.5 reduce_sum.245
  15.2 6.4 %all-reduce.6 = (f32[8,128]{1,0:T(8,128)S(1)}, f32[128]{0:T(128)S(1)}) all-reduce(f32[8,128]{1,0:T(8,128)S(1)} %reduce_sum.245, f32[128]{0:T(128)S(1)} %reduce_sum.254), channel_id=1, replica_groups=mesh['scen'=2,'region'=4,'dest'=4] {'dest'}, use_global_device_ids=true, to_apply=%region_1.2 | all-reduce | flops 1152 | bytes 9216 | tf_op jit(solution)/shard_map/psum | solution.py:67
  22.9 4.8 %all-to-all-start.1 = ((s32[4,1,64]{2,1,0:T(1,128)}), s32[4,1,64]{2,1,0:T(1,128)S(1)}, u32[]{:S(2)}, u32[]{:S(2)}) async-start(s32[4,1,64]{2,1,0:T(1,128)} %all_to_all.86), calls=%async_computation.1 | async-start | bytes 4096 | tf_op jit(solution)/shard_map/all_to_all | solution.py:53
  29.1 4.1 %all-to-all-done.1 = s32[4,1,64]{2,1,0:T(1,128)S(1)} async-done(((s32[4,1,64]{2,1,0:T(1,128)}), s32[4,1,64]{2,1,0:T(1,128)S(1)}, u32[]{:S(2)}, u32[]{:S(2)}) %all-to-all-start.1) | async-done | bytes 1056 | tf_op jit(solution)/shard_map/all_to_all | solution.py:53
  34.2 1.9 gather_fusion
  36.8 3.2 %all-to-all-start.2 = ((f32[4,1,64]{2,1,0:T(1,128)}), f32[4,1,64]{2,1,0:T(1,128)S(1)}, u32[]{:S(2)}, u32[]{:S(2)}) async-start(f32[4,1,64]{2,1,0:T(1,128)} %all_to_all.88), calls=%async_computation.2 | async-start | bytes 4096 | tf_op jit(solution)/shard_map/all_to_all | solution.py:83
  40.2 3.3 %gather_fusion.2 = f32[512]{0:T(512)S(1)} fusion(f32[128]{0:T(128)S(1)} %get-tuple-element.23, s32[1024]{0:T(1024)S(1)} %pad_clamp_fusion), kind=kCustom, calls=%fused_computation.2 | custom fusion | bytes 6144 | tf_op jit(solution)/shard_map/gather | solution.py:86
  43.7 1.7 all-to-all-done.2
  45.4 4.8 %gather_fusion.1 = f32[512]{0:T(512)S(1)} fusion(f32[4,64]{1,0:T(4,128)S(1)} %bitcast.88, s32[512]{0:T(512)S(1)} %bitcast.76), kind=kCustom, calls=%fused_computation.1 | custom fusion | bytes 8192 | tf_op jit(solution)/shard_map/gather | solution.py:86
  51.6 3.3 %all-to-all-start.5 = ((f32[4,1,64]{2,1,0:T(1,128)}), f32[4,1,64]{2,1,0:T(1,128)S(1)}, u32[]{:S(2)}, u32[]{:S(2)}) async-start(f32[4,1,64]{2,1,0:T(1,128)} %all_to_all.95), calls=%async_computation.5 | async-start | bytes 4096 | tf_op jit(solution)/shard_map/all_to_all | solution.py:100
  55.1 5.3 %all-to-all-done.5 = f32[4,1,64]{2,1,0:T(1,128)S(1)} async-done(((f32[4,1,64]{2,1,0:T(1,128)}), f32[4,1,64]{2,1,0:T(1,128)S(1)}, u32[]{:S(2)}, u32[]{:S(2)}) %all-to-all-start.5) | async-done | bytes 1056 | tf_op jit(solution)/shard_map/all_to_all | solution.py:100
  61.8 1.9 gather_fusion.3
  64.4 3.2 %all-to-all-start.3 = ((f32[4,1,64]{2,1,0:T(1,128)}), f32[4,1,64]{2,1,0:T(1,128)S(1)}, u32[]{:S(2)}, u32[]{:S(2)}) async-start(f32[4,1,64]{2,1,0:T(1,128)} %all_to_all.91), calls=%async_computation.3 | async-start | bytes 4096 | tf_op jit(solution)/shard_map/all_to_all | solution.py:84
  67.7 1.7 gather_fusion.6
  69.4 3.6 %all-to-all-done.3 = f32[4,1,64]{2,1,0:T(1,128)S(1)} async-done(((f32[4,1,64]{2,1,0:T(1,128)}), f32[4,1,64]{2,1,0:T(1,128)S(1)}, u32[]{:S(2)}, u32[]{:S(2)}) %all-to-all-start.3) | async-done | bytes 1056 | tf_op jit(solution)/shard_map/all_to_all | solution.py:84
  73.0 3.4 %all-to-all-start.4 = ((f32[4,64,256]{2,1,0:T(8,128)}), f32[4,64,256]{2,1,0:T(8,128)S(1)}, u32[]{:S(2)}, u32[]{:S(2)}) async-start(f32[4,64,256]{2,1,0:T(8,128)} %bitcast.11), calls=%async_computation.4 | async-start | bytes 524288 | tf_op jit(solution)/shard_map/all_to_all | solution.py:82
  76.4 3.3 %gather_fusion.5 = f32[512]{0:T(512)S(1)} fusion(f32[128]{0:T(128)S(1)} %get-tuple-element.19, s32[1024]{0:T(1024)S(1)} %pad_clamp_fusion), kind=kCustom, calls=%fused_computation.5 | custom fusion | bytes 6144 | tf_op jit(solution)/shard_map/gather | solution.py:87
  79.8 1.6 gather_fusion.8
  81.3 1.7 gather_fusion.15
  83.0 1.6 gather_fusion.17
  84.7 1.0 gather.131
  85.7 0.9 gather.146
  86.6 4.8 %gather_fusion.4 = f32[512]{0:T(512)S(1)} fusion(f32[4,64]{1,0:T(4,128)S(1)} %bitcast.85, s32[512]{0:T(512)S(1)} %bitcast.77), kind=kCustom, calls=%fused_computation.4 | custom fusion | bytes 8192 | tf_op jit(solution)/shard_map/gather | solution.py:87
  92.1 3.9 %gather_fusion.7 = f32[512,256]{1,0:T(8,128)S(1)} fusion(f32[4,64,256]{2,1,0:T(8,128)S(1)} %all-to-all-done.4, s32[512]{0:T(512)S(1)} %bitcast.78), kind=kCustom, calls=%fused_computation.7 | custom fusion | bytes 1052672 | tf_op jit(solution)/shard_map/gather | solution.py:89
  96.0 0.9 gather.129
  97.1 1.6 multiply_reduce_fusion.2
  98.9 5.7 %psum.30 = f32[8,128]{1,0:T(8,128)S(1)} all-reduce(f32[8,128]{1,0:T(8,128)S(1)} %fusion.1), channel_id=1, replica_groups=mesh['scen'=2,'region'=4,'dest'=4] {'dest'}, use_global_device_ids=true, to_apply=%region_19.20 | all-reduce | flops 1024 | bytes 8192 | tf_op jit(solution)/shard_map/psum | solution.py:71
  104.6 1.9 gather_fusion.9
  107.2 5.0 %all-to-all-start.6 = ((f32[4,1,64]{2,1,0:T(1,128)}), f32[4,1,64]{2,1,0:T(1,128)S(1)}, u32[]{:S(2)}, u32[]{:S(2)}) async-start(f32[4,1,64]{2,1,0:T(1,128)} %all_to_all.97), calls=%async_computation.6 | async-start | bytes 4096 | tf_op jit(solution)/shard_map/all_to_all | solution.py:83
  112.4 3.3 %gather_fusion.11 = f32[512]{0:T(512)S(1)} fusion(f32[128]{0:T(128)S(1)} %bitcast_divide_fusion.1, s32[1024]{0:T(1024)S(1)} %pad_clamp_fusion), kind=kCustom, calls=%fused_computation.11 | custom fusion | bytes 6144 | tf_op jit(solution)/shard_map/gather | solution.py:86
  115.9 1.8 all-to-all-done.6
  117.7 4.8 %gather_fusion.10 = f32[512]{0:T(512)S(1)} fusion(f32[4,64]{1,0:T(4,128)S(1)} %bitcast.89, s32[512]{0:T(512)S(1)} %bitcast.79), kind=kCustom, calls=%fused_computation.10 | custom fusion | bytes 8192 | tf_op jit(solution)/shard_map/gather | solution.py:86
  123.8 3.3 %all-to-all-start.9 = ((f32[4,1,64]{2,1,0:T(1,128)}), f32[4,1,64]{2,1,0:T(1,128)S(1)}, u32[]{:S(2)}, u32[]{:S(2)}) async-start(f32[4,1,64]{2,1,0:T(1,128)} %all_to_all.104), calls=%async_computation.9 | async-start | bytes 4096 | tf_op jit(solution)/shard_map/all_to_all | solution.py:100
  127.1 5.5 %all-to-all-done.9 = f32[4,1,64]{2,1,0:T(1,128)S(1)} async-done(((f32[4,1,64]{2,1,0:T(1,128)}), f32[4,1,64]{2,1,0:T(1,128)S(1)}, u32[]{:S(2)}, u32[]{:S(2)}) %all-to-all-start.9) | async-done | bytes 1056 | tf_op jit(solution)/shard_map/all_to_all | solution.py:100
  132.6 3.4 %all-to-all-start.8 = ((f32[4,64,256]{2,1,0:T(8,128)}), f32[4,64,256]{2,1,0:T(8,128)S(1)}, u32[]{:S(2)}, u32[]{:S(2)}) async-start(f32[4,64,256]{2,1,0:T(8,128)} %bitcast.20), calls=%async_computation.8 | async-start | bytes 524288 | tf_op jit(solution)/shard_map/all_to_all | solution.py:82
  137.1 1.9 gather_fusion.12
  139.6 3.1 %all-to-all-done.8 = f32[4,64,256]{2,1,0:T(8,128)S(1)} async-done(((f32[4,64,256]{2,1,0:T(8,128)}), f32[4,64,256]{2,1,0:T(8,128)S(1)}, u32[]{:S(2)}, u32[]{:S(2)}) %all-to-all-start.8) | async-done | bytes 262176 | tf_op jit(solution)/shard_map/all_to_all | solution.py:82
  142.7 3.4 %all-to-all-start.7 = ((f32[4,1,64]{2,1,0:T(1,128)}), f32[4,1,64]{2,1,0:T(1,128)S(1)}, u32[]{:S(2)}, u32[]{:S(2)}) async-start(f32[4,1,64]{2,1,0:T(1,128)} %all_to_all.100), calls=%async_computation.7 | async-start | bytes 4096 | tf_op jit(solution)/shard_map/all_to_all | solution.py:84
  146.3 3.9 %gather_fusion.16 = f32[512,256]{1,0:T(8,128)S(1)} fusion(f32[4,64,256]{2,1,0:T(8,128)S(1)} %all-to-all-done.8, s32[512]{0:T(512)S(1)} %bitcast.80), kind=kCustom, calls=%fused_computation.16 | custom fusion | bytes 1052672 | tf_op jit(solution)/shard_map/gather | solution.py:89
  150.4 3.3 %gather_fusion.14 = f32[512]{0:T(512)S(1)} fusion(f32[128]{0:T(128)S(1)} %get-tuple-element.17, s32[1024]{0:T(1024)S(1)} %pad_clamp_fusion), kind=kCustom, calls=%fused_computation.14 | custom fusion | bytes 6144 | tf_op jit(solution)/shard_map/gather | solution.py:87
  153.9 4.8 %gather_fusion.13 = f32[512]{0:T(512)S(1)} fusion(f32[4,64]{1,0:T(4,128)S(1)} %bitcast.87, s32[512]{0:T(512)S(1)} %bitcast.81), kind=kCustom, calls=%fused_computation.13 | custom fusion | bytes 8192 | tf_op jit(solution)/shard_map/gather | solution.py:87
  160.1 5.7 %psum.31 = f32[8,128]{1,0:T(8,128)S(1)} all-reduce(f32[8,128]{1,0:T(8,128)S(1)} %fusion), channel_id=1, replica_groups=mesh['scen'=2,'region'=4,'dest'=4] {'dest'}, use_global_device_ids=true, to_apply=%region_27.28 | all-reduce | flops 1024 | bytes 8192 | tf_op jit(solution)/shard_map/psum | solution.py:71
  165.8 1.9 gather_fusion.18
  168.3 5.1 %all-to-all-start.10 = ((f32[4,1,64]{2,1,0:T(1,128)}), f32[4,1,64]{2,1,0:T(1,128)S(1)}, u32[]{:S(2)}, u32[]{:S(2)}) async-start(f32[4,1,64]{2,1,0:T(1,128)} %all_to_all.106), calls=%async_computation.10 | async-start | bytes 4096 | tf_op jit(solution)/shard_map/all_to_all | solution.py:83
  173.4 3.3 %gather_fusion.20 = f32[512]{0:T(512)S(1)} fusion(f32[128]{0:T(128)S(1)} %bitcast_divide_fusion, s32[1024]{0:T(1024)S(1)} %pad_clamp_fusion), kind=kCustom, calls=%fused_computation.20 | custom fusion | bytes 6144 | tf_op jit(solution)/shard_map/gather | solution.py:86
  176.9 2.0 all-to-all-done.10
  178.9 4.8 %gather_fusion.19 = f32[512]{0:T(512)S(1)} fusion(f32[4,64]{1,0:T(4,128)S(1)} %bitcast.90, s32[512]{0:T(512)S(1)} %bitcast.82), kind=kCustom, calls=%fused_computation.19 | custom fusion | bytes 8192 | tf_op jit(solution)/shard_map/gather | solution.py:86
  185.0 3.2 %all-to-all-start.13 = ((f32[4,1,64]{2,1,0:T(1,128)}), f32[4,1,64]{2,1,0:T(1,128)S(1)}, u32[]{:S(2)}, u32[]{:S(2)}) async-start(f32[4,1,64]{2,1,0:T(1,128)} %all_to_all.113), calls=%async_computation.13 | async-start | bytes 4096 | tf_op jit(solution)/shard_map/all_to_all | solution.py:100
  188.4 5.2 %all-to-all-done.13 = f32[4,1,64]{2,1,0:T(1,128)S(1)} async-done(((f32[4,1,64]{2,1,0:T(1,128)}), f32[4,1,64]{2,1,0:T(1,128)S(1)}, u32[]{:S(2)}, u32[]{:S(2)}) %all-to-all-start.13) | async-done | bytes 1056 | tf_op jit(solution)/shard_map/all_to_all | solution.py:100
  194.5 1.9 gather_fusion.21
  197.1 3.2 %all-to-all-start.11 = ((f32[4,1,64]{2,1,0:T(1,128)}), f32[4,1,64]{2,1,0:T(1,128)S(1)}, u32[]{:S(2)}, u32[]{:S(2)}) async-start(f32[4,1,64]{2,1,0:T(1,128)} %all_to_all.109), calls=%async_computation.11 | async-start | bytes 4096 | tf_op jit(solution)/shard_map/all_to_all | solution.py:84
  200.4 1.7 gather_fusion.24
  202.0 3.7 %all-to-all-done.11 = f32[4,1,64]{2,1,0:T(1,128)S(1)} async-done(((f32[4,1,64]{2,1,0:T(1,128)}), f32[4,1,64]{2,1,0:T(1,128)S(1)}, u32[]{:S(2)}, u32[]{:S(2)}) %all-to-all-start.11) | async-done | bytes 1056 | tf_op jit(solution)/shard_map/all_to_all | solution.py:84
  205.7 3.6 %all-to-all-start.12 = ((f32[4,64,256]{2,1,0:T(8,128)}), f32[4,64,256]{2,1,0:T(8,128)S(1)}, u32[]{:S(2)}, u32[]{:S(2)}) async-start(f32[4,64,256]{2,1,0:T(8,128)} %bitcast.29), calls=%async_computation.12 | async-start | bytes 524288 | tf_op jit(solution)/shard_map/all_to_all | solution.py:82
  209.5 1.6 gather_fusion.26
  211.1 0.9 gather.161
  212.3 3.3 %gather_fusion.23 = f32[512]{0:T(512)S(1)} fusion(f32[128]{0:T(128)S(1)} %get-tuple-element.15, s32[1024]{0:T(1024)S(1)} %pad_clamp_fusion), kind=kCustom, calls=%fused_computation.23 | custom fusion | bytes 6144 | tf_op jit(solution)/shard_map/gather | solution.py:87
  215.7 4.8 %gather_fusion.22 = f32[512]{0:T(512)S(1)} fusion(f32[4,64]{1,0:T(4,128)S(1)} %bitcast.86, s32[512]{0:T(512)S(1)} %bitcast.83), kind=kCustom, calls=%fused_computation.22 | custom fusion | bytes 8192 | tf_op jit(solution)/shard_map/gather | solution.py:87
  220.6 3.9 %gather_fusion.25 = f32[512,256]{1,0:T(8,128)S(1)} fusion(f32[4,64,256]{2,1,0:T(8,128)S(1)} %all-to-all-done.12, s32[512]{0:T(512)S(1)} %bitcast.84), kind=kCustom, calls=%fused_computation.25 | custom fusion | bytes 1052672 | tf_op jit(solution)/shard_map/gather | solution.py:89
  224.6 0.9 gather.159
  225.6 1.6 multiply_reduce_fusion
  227.3 1.0 pad_maximum_fusion.2
  (146 shorter events, 26.2 us)
Async XLA Ops:
  0.0 21.6 %copy-start = (f32[8,128,256]{2,1,0:T(8,128)S(1)}, f32[8,128,256]{2,1,0:T(8,128)}, u32[]{:S(2)}) copy-start(f32[8,128,256]{2,1,0:T(8,128)} %param.6) | copy-start | bytes 3145732
  4.9 18.0 %all-to-all-start = ((s32[4,1,64]{2,1,0:T(1,128)}), s32[4,1,64]{2,1,0:T(1,128)S(1)}, u32[]{:S(2)}, u32[]{:S(2)}) async-start(s32[4,1,64]{2,1,0:T(1,128)} %select_n.421), calls=%async_computation | async-start | bytes 4096 | tf_op jit(solution)/shard_map/all_to_all | solution.py:52
  13.6 1.5 copy-start.4
  22.9 10.3 %all-to-all-start.1 = ((s32[4,1,64]{2,1,0:T(1,128)}), s32[4,1,64]{2,1,0:T(1,128)S(1)}, u32[]{:S(2)}, u32[]{:S(2)}) async-start(s32[4,1,64]{2,1,0:T(1,128)} %all_to_all.86), calls=%async_computation.1 | async-start | bytes 4096 | tf_op jit(solution)/shard_map/all_to_all | solution.py:53
  36.8 8.7 %all-to-all-start.2 = ((f32[4,1,64]{2,1,0:T(1,128)}), f32[4,1,64]{2,1,0:T(1,128)S(1)}, u32[]{:S(2)}, u32[]{:S(2)}) async-start(f32[4,1,64]{2,1,0:T(1,128)} %all_to_all.88), calls=%async_computation.2 | async-start | bytes 4096 | tf_op jit(solution)/shard_map/all_to_all | solution.py:83
  51.6 8.8 %all-to-all-start.5 = ((f32[4,1,64]{2,1,0:T(1,128)}), f32[4,1,64]{2,1,0:T(1,128)S(1)}, u32[]{:S(2)}, u32[]{:S(2)}) async-start(f32[4,1,64]{2,1,0:T(1,128)} %all_to_all.95), calls=%async_computation.5 | async-start | bytes 4096 | tf_op jit(solution)/shard_map/all_to_all | solution.py:100
  64.4 8.6 %all-to-all-start.3 = ((f32[4,1,64]{2,1,0:T(1,128)}), f32[4,1,64]{2,1,0:T(1,128)S(1)}, u32[]{:S(2)}, u32[]{:S(2)}) async-start(f32[4,1,64]{2,1,0:T(1,128)} %all_to_all.91), calls=%async_computation.3 | async-start | bytes 4096 | tf_op jit(solution)/shard_map/all_to_all | solution.py:84
  73.0 19.1 %all-to-all-start.4 = ((f32[4,64,256]{2,1,0:T(8,128)}), f32[4,64,256]{2,1,0:T(8,128)S(1)}, u32[]{:S(2)}, u32[]{:S(2)}) async-start(f32[4,64,256]{2,1,0:T(8,128)} %bitcast.11), calls=%async_computation.4 | async-start | bytes 524288 | tf_op jit(solution)/shard_map/all_to_all | solution.py:82
  96.0 1.0 copy-start.3
  96.0 1.0 copy-start.8
  97.1 1.6 copy-start.5
  107.2 10.5 %all-to-all-start.6 = ((f32[4,1,64]{2,1,0:T(1,128)}), f32[4,1,64]{2,1,0:T(1,128)S(1)}, u32[]{:S(2)}, u32[]{:S(2)}) async-start(f32[4,1,64]{2,1,0:T(1,128)} %all_to_all.97), calls=%async_computation.6 | async-start | bytes 4096 | tf_op jit(solution)/shard_map/all_to_all | solution.py:83
  123.8 8.8 %all-to-all-start.9 = ((f32[4,1,64]{2,1,0:T(1,128)}), f32[4,1,64]{2,1,0:T(1,128)S(1)}, u32[]{:S(2)}, u32[]{:S(2)}) async-start(f32[4,1,64]{2,1,0:T(1,128)} %all_to_all.104), calls=%async_computation.9 | async-start | bytes 4096 | tf_op jit(solution)/shard_map/all_to_all | solution.py:100
  132.6 10.2 %all-to-all-start.8 = ((f32[4,64,256]{2,1,0:T(8,128)}), f32[4,64,256]{2,1,0:T(8,128)S(1)}, u32[]{:S(2)}, u32[]{:S(2)}) async-start(f32[4,64,256]{2,1,0:T(8,128)} %bitcast.20), calls=%async_computation.8 | async-start | bytes 524288 | tf_op jit(solution)/shard_map/all_to_all | solution.py:82
  142.7 11.2 %all-to-all-start.7 = ((f32[4,1,64]{2,1,0:T(1,128)}), f32[4,1,64]{2,1,0:T(1,128)S(1)}, u32[]{:S(2)}, u32[]{:S(2)}) async-start(f32[4,1,64]{2,1,0:T(1,128)} %all_to_all.100), calls=%async_computation.7 | async-start | bytes 4096 | tf_op jit(solution)/shard_map/all_to_all | solution.py:84
  153.9 4.9 %copy-start.1 = (f32[128,4,256]{2,1,0:T(4,128)S(1)}, f32[128,4,256]{2,1,0:T(4,128)}, u32[]{:S(2)}) copy-start(f32[128,4,256]{2,1,0:T(4,128)} %gather.146) | copy-start | bytes 1572868
  158.9 0.9 copy-start.6
  168.3 10.6 %all-to-all-start.10 = ((f32[4,1,64]{2,1,0:T(1,128)}), f32[4,1,64]{2,1,0:T(1,128)S(1)}, u32[]{:S(2)}, u32[]{:S(2)}) async-start(f32[4,1,64]{2,1,0:T(1,128)} %all_to_all.106), calls=%async_computation.10 | async-start | bytes 4096 | tf_op jit(solution)/shard_map/all_to_all | solution.py:83
  185.0 8.7 %all-to-all-start.13 = ((f32[4,1,64]{2,1,0:T(1,128)}), f32[4,1,64]{2,1,0:T(1,128)S(1)}, u32[]{:S(2)}, u32[]{:S(2)}) async-start(f32[4,1,64]{2,1,0:T(1,128)} %all_to_all.113), calls=%async_computation.13 | async-start | bytes 4096 | tf_op jit(solution)/shard_map/all_to_all | solution.py:100
  197.1 8.6 %all-to-all-start.11 = ((f32[4,1,64]{2,1,0:T(1,128)}), f32[4,1,64]{2,1,0:T(1,128)S(1)}, u32[]{:S(2)}, u32[]{:S(2)}) async-start(f32[4,1,64]{2,1,0:T(1,128)} %all_to_all.109), calls=%async_computation.11 | async-start | bytes 4096 | tf_op jit(solution)/shard_map/all_to_all | solution.py:84
  205.7 14.9 %all-to-all-start.12 = ((f32[4,64,256]{2,1,0:T(8,128)}), f32[4,64,256]{2,1,0:T(8,128)S(1)}, u32[]{:S(2)}, u32[]{:S(2)}) async-start(f32[4,64,256]{2,1,0:T(8,128)} %bitcast.29), calls=%async_computation.12 | async-start | bytes 524288 | tf_op jit(solution)/shard_map/all_to_all | solution.py:82
  224.6 1.0 copy-start.2
  225.6 1.6 copy-start.7
where the time goes:
time: 230 us; the launch traced here: 228 us
  local copies, waits for them, and re-layouts  101 us (44%)
  starting transfers between devices  54.7 us (24%)
  waiting for transfers between devices  35.9 us (16%)
  other arithmetic  18.3 us (8%)
  blocking collectives  17.7 us (8%)
    all_to_all x3, waiting for transfers between devices, local(): lax.all_to_all(send_back, 'region', split_axis=0, concat_axis=0, tiled=True)  15.9 us
    gather x6, local copies, waits for them, and re-layouts, local(): got_unit[pick_peer, pick_slot]  14.6 us
    gather x6, local copies, waits for them, and re-layouts, local(): got_count[pick_peer, pick_slot]  14.6 us
    gather x6, local copies, waits for them, and re-layouts, local(): got_rows[pick_peer, pick_slot]  13.8 us
    all_to_all x3, starting transfers between devices, local(): lax.all_to_all(sent_count, 'region', split_axis=0, concat_axis=0, tiled=T...  13.4 us
    psum x2, blocking collectives, local(): cell_sum = lax.psum(jnp.sum(density, axis=2), 'dest')  11.3 us
    all_to_all x3, starting transfers between devices, local(): lax.all_to_all(sent_rows, 'region', split_axis=0, concat_axis=0, tiled=True)  10.4 us
    gather x6, local copies, waits for them, and re-layouts, local(): unit_share[local_ids]  10.4 us
  transfers between devices with their start and end apart: 14, of which 10 were waited for; matrix products, arithmetic and copies ran while one was open for 25% of the time, Pallas kernels for 0%

commit v1 on v0

--- a/solution.py
+++ b/solution.py
@@ -1,6 +1,10 @@
+import functools
+
 import jax
 import jax.numpy as jnp
 from jax import lax
+from jax.experimental import pallas as pl
+from jax.experimental.pallas import tpu as pltpu
 from jax.sharding import PartitionSpec as P
 
 COMM = 1024
@@ -26,7 +30,7 @@
     return jnp.sum(jnp.where(member, ranked, 0), axis=1)
 
 
-def local(density, anchor, feeds, turns, plan, capacity_levels):
+def stepwise(density, anchor, feeds, turns, plan, capacity_levels):
     num_cells, num_links, commodity_width = density.shape
     peers = lax.axis_size("region")
     my_region = lax.axis_index("region")
@@ -119,6 +123,292 @@
     return density
 
 
+def split_two(values):
+    high = values.astype(jnp.bfloat16)
+    low = (values - high.astype(jnp.float32)).astype(jnp.bfloat16)
+    return high, low
+
+
+def dot(a, b, dims):
+    return lax.dot_general(a, b, (dims, ((), ())), preferred_element_type=jnp.float32)
+
+
+NN = ((1,), (0,))
+NT = ((1,), (1,))
+
+
+def vector_dot(row, matrix, dims):
+    first = row.astype(jnp.bfloat16).astype(jnp.float32)
+    second = (row - first).astype(jnp.bfloat16).astype(jnp.float32)
+    third = row - first - second
+    at = lax.broadcasted_iota(jnp.int32, (16, row.shape[1]), 0)
+    stacked = jnp.where(at == 0, first, jnp.where(at == 1, second, jnp.where(at == 2, third, 0.0)))
+    return jnp.sum(dot(stacked.astype(jnp.bfloat16), matrix, dims), axis=0, keepdims=True)
+
+
+def network_kernel(
+    regions, shares, slots, steps,
+    density_ref, anchor_ref, ints_ref, levels_ref, out_ref,
+    ints_all, parts, totals, matrix, keys, rows_out, rows_in, weights, coefs, columns,
+    int_send, int_recv, part_send, part_recv, total_send, total_recv, row_send, row_recv,
+):
+    cells, links, width = density_ref.shape
+    all_links = regions * links
+    held = regions * slots
+    me = lax.axis_index("region")
+    share = lax.axis_index("dest")
+    mine = pl.ds(pl.multiple_of(me * links, links), links)
+
+    def region_at(offset):
+        return lax.rem(me + offset, regions)
+
+    def lanes(region):
+        return pl.ds(pl.multiple_of(region * links, links), links)
+
+    def slot_rows(region):
+        return pl.ds(pl.multiple_of(region * slots, slots), slots)
+
+    def to_region(src, dst, send, recv, offset):
+        return pltpu.make_async_remote_copy(
+            src_ref=src, dst_ref=dst, send_sem=send.at[offset], recv_sem=recv.at[offset],
+            device_id={"region": region_at(offset)}, device_id_type=pl.DeviceIdType.MESH,
+        )
+
+    barrier = pltpu.get_barrier_semaphore()
+    for offset in range(1, regions):
+        pl.semaphore_signal(barrier, inc=1, device_id={"region": region_at(offset)}, device_id_type=pl.DeviceIdType.MESH)
+    for offset in range(1, shares):
+        pl.semaphore_signal(
+            barrier, inc=1, device_id={"dest": lax.rem(share + offset, shares)}, device_id_type=pl.DeviceIdType.MESH
+        )
+
+    ints_all[:, mine] = ints_ref[...]
+    summed = jnp.zeros((16, links), jnp.float32)
+    pick = lax.broadcasted_iota(jnp.int32, (16, width), 0)
+    for cell in range(cells + 1):
+        high, low = split_two(density_ref[cell] if cell < cells else anchor_ref[...])
+        ones = jnp.where(pick == cell, 1.0, 0.0).astype(jnp.bfloat16)
+        summed = summed + dot(ones, high, NT) + dot(ones, low, NT)
+    parts[share] = summed
+    rows_in[:, slot_rows(me), :] = jnp.zeros((steps, slots, width), jnp.float32)
+    coefs[...] = jnp.zeros_like(coefs)
+
+    pl.semaphore_wait(barrier, regions + shares - 2)
+    int_copies, part_copies, total_copies, row_copies = [], [], [], []
+    for offset in range(1, regions):
+        copy = to_region(ints_all.at[:, mine], ints_all.at[:, mine], int_send, int_recv, offset)
+        copy.start()
+        int_copies.append(copy)
+    for offset in range(1, shares):
+        copy = pltpu.make_async_remote_copy(
+            src_ref=parts.at[share], dst_ref=parts.at[share],
+            send_sem=part_send.at[offset], recv_sem=part_recv.at[offset],
+            device_id={"dest": lax.rem(share + offset, shares)}, device_id_type=pl.DeviceIdType.MESH,
+        )
+        copy.start()
+        part_copies.append(copy)
+
+    for copy in int_copies:
+        copy.wait()
+    for block in range(regions):
+        named = lax.broadcasted_iota(jnp.int32, (links, all_links), 0) + block * links
+        count = jnp.zeros((links, all_links), jnp.float32)
+        for entry in range(4):
+            count = count + jnp.where(
+                ints_all[entry : entry + 1, :] == named, ints_all[4 + entry : 5 + entry, :].astype(jnp.float32), 0.0
+            )
+        matrix[block * links : (block + 1) * links, :] = count.astype(jnp.bfloat16)
+
+    region_row = lax.broadcasted_iota(jnp.int32, (16, all_links), 0)
+    link_column = lax.broadcasted_iota(jnp.int32, (16, all_links), 1)
+    member = jnp.where(link_column // links == region_row, 1.0, 0.0).astype(jnp.bfloat16)
+    taken = dot(member, matrix[...], NT)
+    denominator = jnp.sum(taken, axis=0, keepdims=True) + EXIT_WEIGHT
+    before = lax.broadcasted_iota(jnp.int32, (links, links), 0) < lax.broadcasted_iota(jnp.int32, (links, links), 1)
+    before = jnp.where(before, 1.0, 0.0).astype(jnp.bfloat16)
+    named_at = jnp.where(taken > 0.0, 1.0, 0.0)
+    for block in range(regions):
+        at = slice(block * links, (block + 1) * links)
+        rank = dot(named_at[:, at].astype(jnp.bfloat16), before, NN)
+        keys[:, at] = jnp.where(named_at[:, at] > 0.0, rank, -1.0)
+
+    for copy in part_copies:
+        copy.wait()
+    total_here = parts[0]
+    for other in range(1, shares):
+        total_here = total_here + parts[other]
+    totals[:, mine] = total_here
+    for offset in range(1, regions):
+        copy = to_region(totals.at[:, mine], totals.at[:, mine], total_send, total_recv, offset)
+        copy.start()
+        total_copies.append(copy)
+
+    own_keys = keys[:, mine]
+    slot_at = lax.broadcasted_iota(jnp.int32, (slots, links), 0).astype(jnp.float32)
+    chosen = jnp.concatenate(
+        [jnp.where(own_keys[region : region + 1] == slot_at, 1.0, 0.0) for region in range(regions)], axis=0
+    ).astype(jnp.bfloat16)
+    for back in range(steps):
+        high, low = split_two(density_ref[cells - 1 - back])
+        rows_out[back] = dot(chosen, high, NN) + dot(chosen, low, NN)
+    for offset in range(1, regions):
+        copy = to_region(
+            rows_out.at[:, slot_rows(region_at(offset)), :], rows_in.at[:, slot_rows(me), :], row_send, row_recv, offset
+        )
+        copy.start()
+        row_copies.append(copy)
+
+    wanted = jnp.sum(jnp.where(region_row == me, keys[...], 0.0), axis=0, keepdims=True)
+    lane = lax.broadcasted_iota(jnp.int32, (1, all_links), 1)
+    wanted = jnp.where(
+        (wanted >= 0.0) & (lane // links != me), wanted + (lane // links * slots).astype(jnp.float32), -1.0
+    )
+    held_at = jnp.where(
+        lax.broadcasted_iota(jnp.int32, (held, all_links), 0).astype(jnp.float32) == wanted, 1.0, 0.0
+    ).astype(jnp.bfloat16)
+    far_counts = jnp.transpose(dot(held_at, matrix[:, mine], NN))
+    near_counts = jnp.transpose(matrix[mine, mine].astype(jnp.float32))
+
+    for copy in total_copies:
+        copy.wait()
+    cell_row = lax.broadcasted_iota(jnp.int32, (cells, all_links), 0)
+
+    def moved_up(values):
+        return jnp.where(cell_row == 0, 0.0, pltpu.roll(values, 1, 0))
+
+    total = totals[0:cells, :]
+    anchor_total = totals[cells : cells + 1, :]
+    kept = [jnp.ones((cells, all_links), jnp.float32)]
+    entered = []
+    weight_rows = []
+    for step in range(steps):
+        plan_row = ints_all[8 + step : 9 + step, :]
+        capacity = jnp.zeros((1, all_links), jnp.float32)
+        for level in range(levels_ref.shape[0]):
+            capacity = jnp.where(plan_row == level, levels_ref[level], capacity)
+        capacity = capacity * COMM
+        sending = jnp.minimum(FREE_SPEED * total, capacity)
+        receiving = jnp.minimum(capacity, WAVE_SPEED * (JAM_FACTOR * COMM - total))
+        per_count = sending[cells - 1 : cells] / denominator
+        unit_share = per_count / total[cells - 1 : cells]
+        demand = vector_dot(per_count, matrix[...], NN) + anchor_total
+        ratio = receiving[0:1] / jnp.maximum(receiving[0:1], demand)
+        passed = vector_dot(ratio, matrix[...], NT)
+        leaving = unit_share * (passed + EXIT_WEIGHT)
+        through = jnp.where(cell_row < cells - 1, jnp.minimum(sending, pltpu.roll(receiving, cells - 1, 0)), 0.0)
+        going = through / total
+        staying = 1.0 - going - jnp.where(cell_row == cells - 1, leaving, 0.0)
+        weight_rows += [unit_share * part[cells - 1 : cells] for part in kept]
+        total = (
+            total - through + moved_up(through)
+            + jnp.where(cell_row == 0, ratio * demand, 0.0)
+            - jnp.where(cell_row == cells - 1, leaving * total, 0.0)
+        )
+        zero = jnp.zeros((cells, all_links), jnp.float32)
+        kept = [
+            staying * same + moved_up(going * above) for same, above in zip(kept + [zero], [zero] + kept)
+        ]
+        entered = [staying * part + moved_up(going * part) for part in entered]
+        entered.append(jnp.where(cell_row == 0, ratio, 0.0))
+
+    for index, row in enumerate(weight_rows):
+        weights[index : index + 1, :] = row
+    blocks = kept + entered + [functools.reduce(lambda a, b: a + b, entered)]
+    for index, block in enumerate(blocks):
+        coefs[index * cells : (index + 1) * cells, :] = block
+    columns[...] = jnp.transpose(coefs[:, mine])
+
+    def column(block, cell):
+        at = block * cells + cell
+        return columns[:, at : at + 1]
+
+    weight_high, weight_low = split_two(weights[...])
+    far_weights = dot(weight_high, held_at, NT) + dot(weight_low, held_at, NT)
+    near_weights = weights[:, mine]
+
+    def mixed(counts, row_weights, content):
+        results = []
+        for step in range(steps):
+            gathered = None
+            for back in range(step + 1):
+                index = step * (step + 1) // 2 + back
+                high, low = split_two(counts * row_weights[index : index + 1])
+                content_high, content_low = content[back]
+                term = dot(high, content_high, NN) + dot(low, content_high, NN) + dot(high, content_low, NN)
+                gathered = term if gathered is None else gathered + term
+            results.append(gathered)
+        return results
+
+    near = mixed(near_counts, near_weights, [split_two(density_ref[cells - 1 - back]) for back in range(steps)])
+    for cell in range(cells - 1, -1, -1):
+        value = column(0, cell) * density_ref[cell]
+        for back in range(1, min(steps, cell) + 1):
+            value = value + column(back, cell) * density_ref[cell - back]
+        if cell < steps:
+            value = value + column(2 * steps + 1, cell) * anchor_ref[...]
+            for step in range(steps - cell):
+                value = value + column(steps + 1 + step, cell) * near[step]
+        out_ref[cell] = value
+
+    for copy in row_copies:
+        copy.wait()
+    far = mixed(far_counts, far_weights, [split_two(rows_in[back]) for back in range(steps)])
+    for cell in range(steps):
+        value = out_ref[cell]
+        for step in range(steps - cell):
+            value = value + column(steps + 1 + step, cell) * far[step]
+        out_ref[cell] = value
+
+
+def fused(density, anchor, feeds, turns, plan, capacity_levels):
+    cells, links, width = density.shape
+    steps = plan.shape[0]
+    regions = lax.axis_size("region")
+    shares = lax.axis_size("dest")
+    slots = slot_bound(links, regions)
+    all_links = regions * links
+    ints = jnp.concatenate(
+        [feeds.T, turns.T, plan, jnp.zeros((8 - steps, links), jnp.int32)], axis=0
+    )
+    vmem = pl.BlockSpec(memory_space=pltpu.VMEM)
+    return pl.pallas_call(
+        functools.partial(network_kernel, regions, shares, slots, steps),
+        out_shape=jax.ShapeDtypeStruct(density.shape, jnp.float32),
+        in_specs=[vmem, vmem, vmem, pl.BlockSpec(memory_space=pltpu.SMEM)],
+        out_specs=vmem,
+        scratch_shapes=[
+            pltpu.VMEM((16, all_links), jnp.int32),
+            pltpu.VMEM((shares, 16, links), jnp.float32),
+            pltpu.VMEM((16, all_links), jnp.float32),
+            pltpu.VMEM((all_links, all_links), jnp.bfloat16),
+            pltpu.VMEM((16, all_links), jnp.float32),
+            pltpu.VMEM((steps, regions * slots, width), jnp.float32),
+            pltpu.VMEM((steps, regions * slots, width), jnp.float32),
+            pltpu.VMEM((8, all_links), jnp.float32),
+            pltpu.VMEM((128, all_links), jnp.float32),
+            pltpu.VMEM((links, 128), jnp.float32),
+        ]
+        + [pltpu.SemaphoreType.DMA((regions,))] * 2
+        + [pltpu.SemaphoreType.DMA((shares,))] * 2
+        + [pltpu.SemaphoreType.DMA((regions,))] * 4,
+        compiler_params=pltpu.CompilerParams(
+            collective_id=0, has_side_effects=True, vmem_limit_bytes=32 * 1024 * 1024
+        ),
+    )(density, anchor, ints, capacity_levels)
+
+
+def slot_bound(links, regions):
+    return 4 * max(1, (links // 2 + 4 * (regions - 2) - 1) // (4 * (regions - 2)))
+
+
+def local(density, *rest):
+    regions = lax.axis_size("region")
+    links = density.shape[1]
+    if regions * links <= 1024 and regions * slot_bound(links, regions) == 128:
+        return fused(density, *rest)
+    return stepwise(density, *rest)
+
+
 def solution(mesh):
     in_specs = (
         P(None, ("scen", "region"), "dest"),

time: 230 us -> 24.2 us (0.11)
  local copies, waits for them, and re-layouts: 101 us -> 4.39 us
  starting transfers between devices: 54.7 us -> 0 us
  waiting for transfers between devices: 35.9 us -> 0 us
  Pallas kernels: 0 us -> 19.5 us
  other arithmetic: 18.3 us -> 0.07 us
  blocking collectives: 17.7 us -> 0 us
    gather x45 -> x0, local copies, waits for them, and re-layouts: 87.4 us -> none  [the longest x6 14.6 us: local(): got_unit[pick_peer, pick_slot]]
    all_to_all x14 -> x0, starting transfers between devices: 54.7 us -> none  [the longest x3 13.4 us: local(): lax.all_to_all(sent_count, 'region', split_axis=0, concat_axis=0, tiled=T...]
    all_to_all x14 -> x0, waiting for transfers between devices: 35.9 us -> none  [the longest x3 15.9 us: local(): lax.all_to_all(send_back, 'region', split_axis=0, concat_axis=0, tiled=True)]
    pallas_call x0 -> x1, Pallas kernels: none -> 19.5 us  [fused(): pl.pallas_call(functools.partial(network_kernel, regions, shares, slots,...]
    psum x3 -> x0, blocking collectives: 17.7 us -> none  [the longest x2 11.3 us: local(): cell_sum = lax.psum(jnp.sum(density, axis=2), 'dest')]
    reduce_sum x24 -> x0, other arithmetic: 9.06 us -> none  [the longest x3 3.55 us: local(): jnp.sum(mixing[:, :, None] * pair_rows.reshape(num_links, 4, commodity_wi...]
    all_to_all x12 -> x0, local copies, waits for them, and re-layouts: 7.75 us -> none  [the longest x4 2.52 us: local(): lax.all_to_all(send_back, 'region', split_axis=0, concat_axis=0, tiled=True)]
    all_to_all x5 -> x0, other arithmetic: 3.38 us -> none  [the longest x3 1.96 us: local(): lax.all_to_all(send_back, 'region', split_axis=0, concat_axis=0, tiled=True)]
  transfers between devices with their start and end apart: 14 -> 0, of which waited for: 10 -> 0; matrix products, arithmetic and copies ran while one was open for 25% -> 0% of each run, Pallas kernels for 0% -> 0%
where the time goes in v1:
time: 24.2 us; the launch traced here: 24 us
  Pallas kernels  19.5 us (81%)
  local copies, waits for them, and re-layouts  4.39 us (18%)
    pallas_call x1, Pallas kernels, fused(): pl.pallas_call(functools.partial(network_kernel, regions, shares, slots,...  19.5 us
    unnamed x13, local copies, waits for them, and re-layouts  4.31 us

profile of v1, /device:TPU:0, one launch (start us, length us, event | category | flops | bytes accessed | tf_op | source)
XLA Modules:
  0.0 24.0 jit_solution(5534355238316283292)
XLA Ops:
  0.0 0.0 copy-start.5
  0.0 0.0 copy-start.4
  0.0 0.0 copy-start.3
  0.0 0.1 pad.3.clone
  0.1 0.6 %copy-done.5 = s32[128,4]{0,1:T(4,128)S(1)} copy-done((s32[128,4]{0,1:T(4,128)S(1)}, s32[128,4]{0,1:T(4,128)}, u32[]{:S(2)}) %copy-start.5) | copy-done | bytes 2072
  0.7 0.0 copy-done.4
  0.7 0.0 copy-done.3
  0.7 0.0 copy-start.2
  0.7 0.1 add_add_fusion.ints_ref
  0.8 0.6 %copy-done.2 = f32[8]{0:T(128)S(1)} copy-done((f32[8]{0:T(128)S(1)}, f32[8]{0:T(128)}, u32[]{:S(2)}) %copy-start.2) | copy-done | bytes 56
  1.4 0.0 copy-start
  1.4 1.2 %copy-done = f32[8,128,256]{2,1,0:T(8,128)S(1)} copy-done((f32[8,128,256]{2,1,0:T(8,128)S(1)}, f32[8,128,256]{2,1,0:T(8,128)}, u32[]{:S(2)}) %copy-start) | copy-done | bytes 1048600
  2.6 0.0 copy-start.1
  2.6 0.9 %copy-done.1 = f32[128,256]{1,0:T(8,128)S(1)} copy-done((f32[128,256]{1,0:T(8,128)S(1)}, f32[128,256]{1,0:T(8,128)}, u32[]{:S(2)}) %copy-start.1) | copy-done | bytes 131096
  3.5 19.5 %shard_map.64 = f32[8,128,256]{2,1,0:T(8,128)S(1)} custom-call(f32[8,128,256]{2,1,0:T(8,128)S(1)} %copy-done, f32[128,256]{1,0:T(8,128)S(1)} %copy-done.1, s32[16,128]{1,0:T(8,128)S(1)} %add_add_fusion.ints_ref, f32[8]{0:T(128)S(1)} %copy-done.2), custom_call_target="tpu_custom_call" | custom-call | tf_op jit(solution)/shard_map/pallas_call | solution.py:374
  23.0 1.0 %copy.8 = f32[8,128,256]{2,1,0:T(8,128)} copy(f32[8,128,256]{2,1,0:T(8,128)S(1)} %shard_map.64) | data formatting | bytes 2097152
  (1 shorter events, 0.0 us)
Async XLA Ops:
  0.0 0.7 %copy-start.5 = (s32[128,4]{0,1:T(4,128)S(1)}, s32[128,4]{0,1:T(4,128)}, u32[]{:S(2)}) copy-start(s32[128,4]{0,1:T(4,128)} %param.8) | copy-start | bytes 6148
  0.0 0.7 %copy-start.4 = (s32[128,4]{0,1:T(4,128)S(1)}, s32[128,4]{0,1:T(4,128)}, u32[]{:S(2)}) copy-start(s32[128,4]{0,1:T(4,128)} %param.9) | copy-start | bytes 6148
  0.0 0.7 %copy-start.3 = (s32[3,128]{1,0:T(4,128)S(1)}, s32[3,128]{1,0:T(4,128)}, u32[]{:S(2)}) copy-start(s32[3,128]{1,0:T(4,128)} %param.10) | copy-start | bytes 4612
  0.7 0.7 %copy-start.2 = (f32[8]{0:T(128)S(1)}, f32[8]{0:T(128)}, u32[]{:S(2)}) copy-start(f32[8]{0:T(128)} %levels_ref.1) | copy-start | bytes 100
  1.4 1.2 %copy-start = (f32[8,128,256]{2,1,0:T(8,128)S(1)}, f32[8,128,256]{2,1,0:T(8,128)}, u32[]{:S(2)}) copy-start(f32[8,128,256]{2,1,0:T(8,128)} %density_ref.1) | copy-start | bytes 3145732
  2.6 0.9 %copy-start.1 = (f32[128,256]{1,0:T(8,128)S(1)}, f32[128,256]{1,0:T(8,128)}, u32[]{:S(2)}) copy-start(f32[128,256]{1,0:T(8,128)} %anchor_ref.1) | copy-start | bytes 393220

commit v2 on v1

--- a/solution.py
+++ b/solution.py
@@ -146,21 +146,27 @@
     return jnp.sum(dot(stacked.astype(jnp.bfloat16), matrix, dims), axis=0, keepdims=True)
 
 
+def across(index, mask):
+    bit = 1
+    while bit <= mask:
+        if mask & bit:
+            index = index + bit - 2 * bit * lax.rem(index // bit, 2)
+        bit *= 2
+    return index
+
+
 def network_kernel(
     regions, shares, slots, steps,
-    density_ref, anchor_ref, ints_ref, levels_ref, out_ref,
-    ints_all, parts, totals, matrix, keys, rows_out, rows_in, weights, coefs, columns,
-    int_send, int_recv, part_send, part_recv, total_send, total_recv, row_send, row_recv,
+    density_hbm, anchor_hbm, feeds_hbm, turns_hbm, plan_hbm, levels_hbm, out_hbm,
+    density_ref, anchor_ref, feeds_ref, turns_ref, plan_ref, levels_ref, out_ref,
+    ints_all, asking, asked, parts, totals, matrix, keys, rows_out, rows_in, weights, coefs, columns,
+    in_sem, out_sem, int_send, int_recv, key_send, key_recv, part_send, part_recv, total_send, total_recv, row_send, row_recv,
 ):
     cells, links, width = density_ref.shape
     all_links = regions * links
     held = regions * slots
     me = lax.axis_index("region")
     share = lax.axis_index("dest")
-    mine = pl.ds(pl.multiple_of(me * links, links), links)
-
-    def region_at(offset):
-        return lax.rem(me + offset, regions)
 
     def lanes(region):
         return pl.ds(pl.multiple_of(region * links, links), links)
@@ -168,109 +174,142 @@
     def slot_rows(region):
         return pl.ds(pl.multiple_of(region * slots, slots), slots)
 
-    def to_region(src, dst, send, recv, offset):
+    mine = lanes(me)
+
+    def start_all(copies):
+        for copy in copies:
+            copy.start()
+        return copies
+
+    def wait_all(copies):
+        for copy in copies:
+            copy.wait()
+
+    def to_region(src, dst, send, recv, mask):
         return pltpu.make_async_remote_copy(
-            src_ref=src, dst_ref=dst, send_sem=send.at[offset], recv_sem=recv.at[offset],
-            device_id={"region": region_at(offset)}, device_id_type=pl.DeviceIdType.MESH,
-        )
+            src_ref=src, dst_ref=dst, send_sem=send.at[mask], recv_sem=recv.at[mask],
+            device_id={"region": across(me, mask)}, device_id_type=pl.DeviceIdType.MESH,
+        )
+
+    masks = list(range(regions // 2, regions)) + list(range(regions // 2 - 1, 0, -1))
 
     barrier = pltpu.get_barrier_semaphore()
-    for offset in range(1, regions):
-        pl.semaphore_signal(barrier, inc=1, device_id={"region": region_at(offset)}, device_id_type=pl.DeviceIdType.MESH)
-    for offset in range(1, shares):
-        pl.semaphore_signal(
-            barrier, inc=1, device_id={"dest": lax.rem(share + offset, shares)}, device_id_type=pl.DeviceIdType.MESH
-        )
-
-    ints_all[:, mine] = ints_ref[...]
+    for mask in masks:
+        pl.semaphore_signal(barrier, inc=1, device_id={"region": across(me, mask)}, device_id_type=pl.DeviceIdType.MESH)
+    for mask in range(1, shares):
+        pl.semaphore_signal(barrier, inc=1, device_id={"dest": across(share, mask)}, device_id_type=pl.DeviceIdType.MESH)
+
+    small = start_all([
+        pltpu.make_async_copy(src, dst, in_sem.at[at]) for at, (src, dst) in enumerate(
+            [(feeds_hbm, feeds_ref), (turns_hbm, turns_ref), (plan_hbm, plan_ref), (levels_hbm, levels_ref)])
+    ])
+    anchor_copy = pltpu.make_async_copy(anchor_hbm, anchor_ref, in_sem.at[4])
+    cell_copies = {
+        cell: pltpu.make_async_copy(density_hbm.at[cell], density_ref.at[cell], in_sem.at[5 + cell])
+        for cell in range(cells - 1, -1, -1)
+    }
+    start_all(list(cell_copies.values()) + [anchor_copy])
+    rows_in[:, slot_rows(me), :] = jnp.zeros((steps, slots, width), jnp.float32)
+    asked[me] = jnp.full((8, links), -1.0, jnp.float32)
+    coefs[...] = jnp.zeros_like(coefs)
+    wait_all(small)
+
+    def counts_of(feeds, turns):
+        named = lax.broadcasted_iota(jnp.int32, (all_links, links), 0)
+        count = jnp.zeros((all_links, links), jnp.float32)
+        for entry in range(4):
+            count = count + jnp.where(
+                feeds[entry : entry + 1] == named, turns[entry : entry + 1].astype(jnp.float32), 0.0
+            )
+        return count.astype(jnp.bfloat16)
+
+    ints_all[0:4, mine] = feeds_ref[...]
+    ints_all[4:8, mine] = turns_ref[...]
+    ints_all[8 : 8 + steps, mine] = plan_ref[...]
+    own_counts = counts_of(feeds_ref[...], turns_ref[...])
+    matrix[:, mine] = own_counts
+    named_at = jnp.where(dot(jnp.ones((16, links), jnp.bfloat16), own_counts, NT) > 0.0, 1.0, 0.0)
+    before = lax.broadcasted_iota(jnp.int32, (links, links), 0) < lax.broadcasted_iota(jnp.int32, (links, links), 1)
+    before = jnp.where(before, 1.0, 0.0).astype(jnp.bfloat16)
+    for block in range(regions):
+        at = slice(block * links, (block + 1) * links)
+        rank = dot(named_at[:, at].astype(jnp.bfloat16), before, NN)
+        key = jnp.where(named_at[:, at] > 0.0, rank, -1.0)
+        keys[:, at] = key
+        asking[block] = key[0:8]
+
     summed = jnp.zeros((16, links), jnp.float32)
     pick = lax.broadcasted_iota(jnp.int32, (16, width), 0)
-    for cell in range(cells + 1):
+    for cell in list(cell_copies) + [cells]:
+        if cell < cells:
+            cell_copies[cell].wait()
+        else:
+            anchor_copy.wait()
         high, low = split_two(density_ref[cell] if cell < cells else anchor_ref[...])
         ones = jnp.where(pick == cell, 1.0, 0.0).astype(jnp.bfloat16)
         summed = summed + dot(ones, high, NT) + dot(ones, low, NT)
     parts[share] = summed
-    rows_in[:, slot_rows(me), :] = jnp.zeros((steps, slots, width), jnp.float32)
-    coefs[...] = jnp.zeros_like(coefs)
 
     pl.semaphore_wait(barrier, regions + shares - 2)
-    int_copies, part_copies, total_copies, row_copies = [], [], [], []
-    for offset in range(1, regions):
-        copy = to_region(ints_all.at[:, mine], ints_all.at[:, mine], int_send, int_recv, offset)
-        copy.start()
-        int_copies.append(copy)
-    for offset in range(1, shares):
-        copy = pltpu.make_async_remote_copy(
+    key_copies = start_all([
+        to_region(asking.at[across(me, mask)], asked.at[me], key_send, key_recv, mask) for mask in masks
+    ])
+    part_copies = start_all([
+        pltpu.make_async_remote_copy(
             src_ref=parts.at[share], dst_ref=parts.at[share],
-            send_sem=part_send.at[offset], recv_sem=part_recv.at[offset],
-            device_id={"dest": lax.rem(share + offset, shares)}, device_id_type=pl.DeviceIdType.MESH,
-        )
-        copy.start()
-        part_copies.append(copy)
-
-    for copy in int_copies:
-        copy.wait()
-    for block in range(regions):
-        named = lax.broadcasted_iota(jnp.int32, (links, all_links), 0) + block * links
-        count = jnp.zeros((links, all_links), jnp.float32)
-        for entry in range(4):
-            count = count + jnp.where(
-                ints_all[entry : entry + 1, :] == named, ints_all[4 + entry : 5 + entry, :].astype(jnp.float32), 0.0
-            )
-        matrix[block * links : (block + 1) * links, :] = count.astype(jnp.bfloat16)
-
-    region_row = lax.broadcasted_iota(jnp.int32, (16, all_links), 0)
-    link_column = lax.broadcasted_iota(jnp.int32, (16, all_links), 1)
-    member = jnp.where(link_column // links == region_row, 1.0, 0.0).astype(jnp.bfloat16)
-    taken = dot(member, matrix[...], NT)
-    denominator = jnp.sum(taken, axis=0, keepdims=True) + EXIT_WEIGHT
-    before = lax.broadcasted_iota(jnp.int32, (links, links), 0) < lax.broadcasted_iota(jnp.int32, (links, links), 1)
-    before = jnp.where(before, 1.0, 0.0).astype(jnp.bfloat16)
-    named_at = jnp.where(taken > 0.0, 1.0, 0.0)
-    for block in range(regions):
-        at = slice(block * links, (block + 1) * links)
-        rank = dot(named_at[:, at].astype(jnp.bfloat16), before, NN)
-        keys[:, at] = jnp.where(named_at[:, at] > 0.0, rank, -1.0)
-
-    for copy in part_copies:
-        copy.wait()
-    total_here = parts[0]
-    for other in range(1, shares):
-        total_here = total_here + parts[other]
-    totals[:, mine] = total_here
-    for offset in range(1, regions):
-        copy = to_region(totals.at[:, mine], totals.at[:, mine], total_send, total_recv, offset)
-        copy.start()
-        total_copies.append(copy)
-
-    own_keys = keys[:, mine]
-    slot_at = lax.broadcasted_iota(jnp.int32, (slots, links), 0).astype(jnp.float32)
-    chosen = jnp.concatenate(
-        [jnp.where(own_keys[region : region + 1] == slot_at, 1.0, 0.0) for region in range(regions)], axis=0
-    ).astype(jnp.bfloat16)
-    for back in range(steps):
-        high, low = split_two(density_ref[cells - 1 - back])
-        rows_out[back] = dot(chosen, high, NN) + dot(chosen, low, NN)
-    for offset in range(1, regions):
-        copy = to_region(
-            rows_out.at[:, slot_rows(region_at(offset)), :], rows_in.at[:, slot_rows(me), :], row_send, row_recv, offset
-        )
-        copy.start()
-        row_copies.append(copy)
-
-    wanted = jnp.sum(jnp.where(region_row == me, keys[...], 0.0), axis=0, keepdims=True)
+            send_sem=part_send.at[mask], recv_sem=part_recv.at[mask],
+            device_id={"dest": across(share, mask)}, device_id_type=pl.DeviceIdType.MESH,
+        )
+        for mask in range(1, shares)
+    ])
+    int_copies = start_all([
+        to_region(ints_all.at[:, mine], ints_all.at[:, mine], int_send, int_recv, mask) for mask in masks
+    ])
+
     lane = lax.broadcasted_iota(jnp.int32, (1, all_links), 1)
+    wanted = keys[0:1, :]
     wanted = jnp.where(
         (wanted >= 0.0) & (lane // links != me), wanted + (lane // links * slots).astype(jnp.float32), -1.0
     )
     held_at = jnp.where(
         lax.broadcasted_iota(jnp.int32, (held, all_links), 0).astype(jnp.float32) == wanted, 1.0, 0.0
     ).astype(jnp.bfloat16)
-    far_counts = jnp.transpose(dot(held_at, matrix[:, mine], NN))
+    far_counts = jnp.transpose(dot(held_at, own_counts, NN))
     near_counts = jnp.transpose(matrix[mine, mine].astype(jnp.float32))
 
-    for copy in total_copies:
-        copy.wait()
+    wait_all(part_copies)
+    total_here = parts[0]
+    for other in range(1, shares):
+        total_here = total_here + parts[other]
+    totals[:, mine] = total_here
+    total_copies = start_all([
+        to_region(totals.at[:, mine], totals.at[:, mine], total_send, total_recv, mask) for mask in masks
+    ])
+
+    wait_all(key_copies)
+    slot_at = lax.broadcasted_iota(jnp.int32, (slots, links), 0).astype(jnp.float32)
+    chosen = jnp.concatenate(
+        [jnp.where(asked[region, 0:1, :] == slot_at, 1.0, 0.0) for region in range(regions)], axis=0
+    ).astype(jnp.bfloat16)
+    row_copies = []
+    for back in range(steps):
+        high, low = split_two(density_ref[cells - 1 - back])
+        rows_out[back] = dot(chosen, high, NN) + dot(chosen, low, NN)
+        row_copies.append(start_all([
+            to_region(
+                rows_out.at[back, slot_rows(across(me, mask)), :], rows_in.at[back, slot_rows(me), :],
+                row_send.at[back], row_recv.at[back], mask,
+            )
+            for mask in masks
+        ]))
+
+    wait_all(int_copies)
+    for mask in masks:
+        theirs = lanes(across(me, mask))
+        matrix[:, theirs] = counts_of(ints_all[0:4, theirs], ints_all[4:8, theirs])
+    denominator = dot(jnp.ones((16, all_links), jnp.bfloat16), matrix[...], NT)[0:1] + EXIT_WEIGHT
+
+    wait_all(total_copies)
     cell_row = lax.broadcasted_iota(jnp.int32, (cells, all_links), 0)
 
     def moved_up(values):
@@ -326,38 +365,48 @@
     far_weights = dot(weight_high, held_at, NT) + dot(weight_low, held_at, NT)
     near_weights = weights[:, mine]
 
-    def mixed(counts, row_weights, content):
-        results = []
-        for step in range(steps):
-            gathered = None
-            for back in range(step + 1):
+    def mixing(counts, row_weights, back):
+        pieces = []
+        for cell in range(steps - back):
+            piece = None
+            for step in range(back, steps - cell):
                 index = step * (step + 1) // 2 + back
-                high, low = split_two(counts * row_weights[index : index + 1])
-                content_high, content_low = content[back]
-                term = dot(high, content_high, NN) + dot(low, content_high, NN) + dot(high, content_low, NN)
-                gathered = term if gathered is None else gathered + term
-            results.append(gathered)
-        return results
-
-    near = mixed(near_counts, near_weights, [split_two(density_ref[cells - 1 - back]) for back in range(steps)])
-    for cell in range(cells - 1, -1, -1):
+                term = column(steps + 1 + step, cell) * row_weights[index : index + 1]
+                piece = term if piece is None else piece + term
+            pieces.append(counts * piece)
+        return split_two(jnp.concatenate(pieces, axis=0))
+
+    def mixed(mixing_pair, content):
+        high, low = mixing_pair
+        content_high, content_low = split_two(content)
+        return dot(high, content_high, NN) + dot(low, content_high, NN) + dot(high, content_low, NN)
+
+    far_mixing = [mixing(far_counts, far_weights, back) for back in range(steps)]
+    near = [
+        mixed(mixing(near_counts, near_weights, back), density_ref[cells - 1 - back]) for back in range(steps)
+    ]
+    out_copies = [
+        pltpu.make_async_copy(out_ref.at[cell], out_hbm.at[cell], out_sem.at[cell]) for cell in range(cells)
+    ]
+    for cell in range(cells):
         value = column(0, cell) * density_ref[cell]
         for back in range(1, min(steps, cell) + 1):
             value = value + column(back, cell) * density_ref[cell - back]
         if cell < steps:
             value = value + column(2 * steps + 1, cell) * anchor_ref[...]
-            for step in range(steps - cell):
-                value = value + column(steps + 1 + step, cell) * near[step]
+            for back in range(steps - cell):
+                value = value + near[back][cell * links : (cell + 1) * links]
         out_ref[cell] = value
-
-    for copy in row_copies:
-        copy.wait()
-    far = mixed(far_counts, far_weights, [split_two(rows_in[back]) for back in range(steps)])
-    for cell in range(steps):
-        value = out_ref[cell]
-        for step in range(steps - cell):
-            value = value + column(steps + 1 + step, cell) * far[step]
-        out_ref[cell] = value
+        if cell >= steps:
+            out_copies[cell].start()
+
+    for back in range(steps):
+        wait_all(row_copies[back])
+        far = mixed(far_mixing[back], rows_in[back])
+        for cell in range(steps - back):
+            out_ref[cell] = out_ref[cell] + far[cell * links : (cell + 1) * links]
+        out_copies[steps - back - 1].start()
+    wait_all(out_copies)
 
 
 def fused(density, anchor, feeds, turns, plan, capacity_levels):
@@ -367,17 +416,23 @@
     shares = lax.axis_size("dest")
     slots = slot_bound(links, regions)
     all_links = regions * links
-    ints = jnp.concatenate(
-        [feeds.T, turns.T, plan, jnp.zeros((8 - steps, links), jnp.int32)], axis=0
-    )
-    vmem = pl.BlockSpec(memory_space=pltpu.VMEM)
+    hbm = pl.BlockSpec(memory_space=pltpu.HBM)
     return pl.pallas_call(
         functools.partial(network_kernel, regions, shares, slots, steps),
         out_shape=jax.ShapeDtypeStruct(density.shape, jnp.float32),
-        in_specs=[vmem, vmem, vmem, pl.BlockSpec(memory_space=pltpu.SMEM)],
-        out_specs=vmem,
+        in_specs=[hbm] * 6,
+        out_specs=hbm,
         scratch_shapes=[
+            pltpu.VMEM(density.shape, jnp.float32),
+            pltpu.VMEM(anchor.shape, jnp.float32),
+            pltpu.VMEM((4, links), jnp.int32),
+            pltpu.VMEM((4, links), jnp.int32),
+            pltpu.VMEM(plan.shape, jnp.int32),
+            pltpu.SMEM(capacity_levels.shape, jnp.float32),
+            pltpu.VMEM(density.shape, jnp.float32),
             pltpu.VMEM((16, all_links), jnp.int32),
+            pltpu.VMEM((regions, 8, links), jnp.float32),
+            pltpu.VMEM((regions, 8, links), jnp.float32),
             pltpu.VMEM((shares, 16, links), jnp.float32),
             pltpu.VMEM((16, all_links), jnp.float32),
             pltpu.VMEM((all_links, all_links), jnp.bfloat16),
@@ -387,14 +442,17 @@
             pltpu.VMEM((8, all_links), jnp.float32),
             pltpu.VMEM((128, all_links), jnp.float32),
             pltpu.VMEM((links, 128), jnp.float32),
+            pltpu.SemaphoreType.DMA((5 + cells,)),
+            pltpu.SemaphoreType.DMA((cells,)),
         ]
+        + [pltpu.SemaphoreType.DMA((regions,))] * 4
+        + [pltpu.SemaphoreType.DMA((shares,))] * 2
         + [pltpu.SemaphoreType.DMA((regions,))] * 2
-        + [pltpu.SemaphoreType.DMA((shares,))] * 2
-        + [pltpu.SemaphoreType.DMA((regions,))] * 4,
+        + [pltpu.SemaphoreType.DMA((steps, regions))] * 2,
         compiler_params=pltpu.CompilerParams(
-            collective_id=0, has_side_effects=True, vmem_limit_bytes=32 * 1024 * 1024
+            collective_id=0, has_side_effects=True, vmem_limit_bytes=60 * 1024 * 1024
         ),
-    )(density, anchor, ints, capacity_levels)
+    )(density, anchor, feeds.T, turns.T, plan, capacity_levels)
 
 
 def slot_bound(links, regions):
@@ -404,7 +462,9 @@
 def local(density, *rest):
     regions = lax.axis_size("region")
     links = density.shape[1]
-    if regions * links <= 1024 and regions * slot_bound(links, regions) == 128:
+    shares = lax.axis_size("dest")
+    even = regions & (regions - 1) == 0 and shares & (shares - 1) == 0
+    if even and regions * links <= 1024 and regions * slot_bound(links, regions) == 128:
         return fused(density, *rest)
     return stepwise(density, *rest)
 

time: 24.2 us -> 23 us (0.950)
  local copies, waits for them, and re-layouts: 4.39 us -> 2.27 us
  Pallas kernels: 19.5 us -> 20.5 us
    unnamed x13 -> x1, local copies, waits for them, and re-layouts: 4.31 us -> 2.27 us
    pallas_call x1, Pallas kernels: 19.5 us -> 20.5 us  [fused(): pl.pallas_call(functools.partial(network_kernel, regions, shares, slots,...]
where the time goes in v2:
time: 23 us; the launch traced here: 22.8 us
  Pallas kernels  20.5 us (89%)
  local copies, waits for them, and re-layouts  2.27 us (10%)
    pallas_call x1, Pallas kernels, fused(): pl.pallas_call(functools.partial(network_kernel, regions, shares, slots,...  20.5 us
    unnamed x1, local copies, waits for them, and re-layouts  2.27 us

profile of v2, /device:TPU:0, one launch (start us, length us, event | category | flops | bytes accessed | tf_op | source)
XLA Modules:
  0.0 22.8 jit_solution(9139970122007226275)
XLA Ops:
  0.0 20.5 %shard_map.64 = f32[8,128,256]{2,1,0:T(8,128)} custom-call(f32[8,128,256]{2,1,0:T(8,128)} %density_hbm.1, f32[128,256]{1,0:T(8,128)} %anchor_hbm.1, s32[4,128]{1,0:T(4,128)} %bitcast.2, s32[4,128]{1,0:T(4,128)} %bitcast.3, s32[3,128]{1,0:T(4,128)} %plan_hbm.1, f32[8]{0:T(128)} %levels_hbm.1), custom_call_target="tpu_custom_call" | custom-call | tf_op jit(solution)/shard_map/pallas_call | solution.py:420
  20.5 2.3 %copy.8 = f32[8,128,256]{2,1,0:T(8,128)} copy(f32[8,128,256]{2,1,0:T(8,128)} %shard_map.64) | data formatting | bytes 2097152

commit v3 on v2

--- a/solution.py
+++ b/solution.py
@@ -157,10 +157,10 @@
 
 def network_kernel(
     regions, shares, slots, steps,
-    density_hbm, anchor_hbm, feeds_hbm, turns_hbm, plan_hbm, levels_hbm, out_hbm,
-    density_ref, anchor_ref, feeds_ref, turns_ref, plan_ref, levels_ref, out_ref,
+    density_hbm, anchor_hbm, feeds_hbm, turns_hbm, plan_hbm, levels_hbm, out_ref,
+    density_ref, anchor_ref, feeds_ref, turns_ref, plan_ref, levels_ref,
     ints_all, asking, asked, parts, totals, matrix, keys, rows_out, rows_in, weights, coefs, columns,
-    in_sem, out_sem, int_send, int_recv, key_send, key_recv, part_send, part_recv, total_send, total_recv, row_send, row_recv,
+    in_sem, int_send, int_recv, key_send, key_recv, part_send, part_recv, total_send, total_recv, row_send, row_recv,
 ):
     cells, links, width = density_ref.shape
     all_links = regions * links
@@ -238,6 +238,14 @@
         keys[:, at] = key
         asking[block] = key[0:8]
 
+    pl.semaphore_wait(barrier, regions + shares - 2)
+    key_copies = start_all([
+        to_region(asking.at[across(me, mask)], asked.at[me], key_send, key_recv, mask) for mask in masks
+    ])
+    int_copies = start_all([
+        to_region(ints_all.at[:, mine], ints_all.at[:, mine], int_send, int_recv, mask) for mask in masks
+    ])
+
     summed = jnp.zeros((16, links), jnp.float32)
     pick = lax.broadcasted_iota(jnp.int32, (16, width), 0)
     for cell in list(cell_copies) + [cells]:
@@ -250,10 +258,6 @@
         summed = summed + dot(ones, high, NT) + dot(ones, low, NT)
     parts[share] = summed
 
-    pl.semaphore_wait(barrier, regions + shares - 2)
-    key_copies = start_all([
-        to_region(asking.at[across(me, mask)], asked.at[me], key_send, key_recv, mask) for mask in masks
-    ])
     part_copies = start_all([
         pltpu.make_async_remote_copy(
             src_ref=parts.at[share], dst_ref=parts.at[share],
@@ -261,29 +265,6 @@
             device_id={"dest": across(share, mask)}, device_id_type=pl.DeviceIdType.MESH,
         )
         for mask in range(1, shares)
-    ])
-    int_copies = start_all([
-        to_region(ints_all.at[:, mine], ints_all.at[:, mine], int_send, int_recv, mask) for mask in masks
-    ])
-
-    lane = lax.broadcasted_iota(jnp.int32, (1, all_links), 1)
-    wanted = keys[0:1, :]
-    wanted = jnp.where(
-        (wanted >= 0.0) & (lane // links != me), wanted + (lane // links * slots).astype(jnp.float32), -1.0
-    )
-    held_at = jnp.where(
-        lax.broadcasted_iota(jnp.int32, (held, all_links), 0).astype(jnp.float32) == wanted, 1.0, 0.0
-    ).astype(jnp.bfloat16)
-    far_counts = jnp.transpose(dot(held_at, own_counts, NN))
-    near_counts = jnp.transpose(matrix[mine, mine].astype(jnp.float32))
-
-    wait_all(part_copies)
-    total_here = parts[0]
-    for other in range(1, shares):
-        total_here = total_here + parts[other]
-    totals[:, mine] = total_here
-    total_copies = start_all([
-        to_region(totals.at[:, mine], totals.at[:, mine], total_send, total_recv, mask) for mask in masks
     ])
 
     wait_all(key_copies)
@@ -302,6 +283,26 @@
             )
             for mask in masks
         ]))
+        if back == 0:
+            wait_all(part_copies)
+            total_here = parts[0]
+            for other in range(1, shares):
+                total_here = total_here + parts[other]
+            totals[:, mine] = total_here
+            total_copies = start_all([
+                to_region(totals.at[:, mine], totals.at[:, mine], total_send, total_recv, mask) for mask in masks
+            ])
+
+    lane = lax.broadcasted_iota(jnp.int32, (1, all_links), 1)
+    wanted = keys[0:1, :]
+    wanted = jnp.where(
+        (wanted >= 0.0) & (lane // links != me), wanted + (lane // links * slots).astype(jnp.float32), -1.0
+    )
+    held_at = jnp.where(
+        lax.broadcasted_iota(jnp.int32, (held, all_links), 0).astype(jnp.float32) == wanted, 1.0, 0.0
+    ).astype(jnp.bfloat16)
+    far_counts = jnp.transpose(dot(held_at, own_counts, NN))
+    near_counts = jnp.transpose(matrix[mine, mine].astype(jnp.float32))
 
     wait_all(int_copies)
     for mask in masks:
@@ -385,9 +386,6 @@
     near = [
         mixed(mixing(near_counts, near_weights, back), density_ref[cells - 1 - back]) for back in range(steps)
     ]
-    out_copies = [
-        pltpu.make_async_copy(out_ref.at[cell], out_hbm.at[cell], out_sem.at[cell]) for cell in range(cells)
-    ]
     for cell in range(cells):
         value = column(0, cell) * density_ref[cell]
         for back in range(1, min(steps, cell) + 1):
@@ -397,16 +395,12 @@
             for back in range(steps - cell):
                 value = value + near[back][cell * links : (cell + 1) * links]
         out_ref[cell] = value
-        if cell >= steps:
-            out_copies[cell].start()
 
     for back in range(steps):
         wait_all(row_copies[back])
         far = mixed(far_mixing[back], rows_in[back])
         for cell in range(steps - back):
             out_ref[cell] = out_ref[cell] + far[cell * links : (cell + 1) * links]
-        out_copies[steps - back - 1].start()
-    wait_all(out_copies)
 
 
 def fused(density, anchor, feeds, turns, plan, capacity_levels):
@@ -421,7 +415,7 @@
         functools.partial(network_kernel, regions, shares, slots, steps),
         out_shape=jax.ShapeDtypeStruct(density.shape, jnp.float32),
         in_specs=[hbm] * 6,
-        out_specs=hbm,
+        out_specs=pl.BlockSpec(memory_space=pltpu.VMEM),
         scratch_shapes=[
             pltpu.VMEM(density.shape, jnp.float32),
             pltpu.VMEM(anchor.shape, jnp.float32),
@@ -429,7 +423,6 @@
             pltpu.VMEM((4, links), jnp.int32),
             pltpu.VMEM(plan.shape, jnp.int32),
             pltpu.SMEM(capacity_levels.shape, jnp.float32),
-            pltpu.VMEM(density.shape, jnp.float32),
             pltpu.VMEM((16, all_links), jnp.int32),
             pltpu.VMEM((regions, 8, links), jnp.float32),
             pltpu.VMEM((regions, 8, links), jnp.float32),
@@ -443,16 +436,15 @@
             pltpu.VMEM((128, all_links), jnp.float32),
             pltpu.VMEM((links, 128), jnp.float32),
             pltpu.SemaphoreType.DMA((5 + cells,)),
-            pltpu.SemaphoreType.DMA((cells,)),
         ]
         + [pltpu.SemaphoreType.DMA((regions,))] * 4
         + [pltpu.SemaphoreType.DMA((shares,))] * 2
         + [pltpu.SemaphoreType.DMA((regions,))] * 2
         + [pltpu.SemaphoreType.DMA((steps, regions))] * 2,
         compiler_params=pltpu.CompilerParams(
-            collective_id=0, has_side_effects=True, vmem_limit_bytes=60 * 1024 * 1024
+            collective_id=0, has_side_effects=True, vmem_limit_bytes=32 * 1024 * 1024
         ),
-    )(density, anchor, feeds.T, turns.T, plan, capacity_levels)
+    )(*(pltpu.with_memory_space_constraint(x, pltpu.HBM) for x in (density, anchor, feeds.T, turns.T, plan, capacity_levels)))
 
 
 def slot_bound(links, regions):

time: 23 us -> 20.9 us (0.909)
  local copies, waits for them, and re-layouts: 2.27 us -> 0.97 us
  Pallas kernels: 20.5 us -> 19.7 us
    unnamed x1, local copies, waits for them, and re-layouts: 2.27 us -> 0.97 us
    pallas_call x1, Pallas kernels: 20.5 us -> 19.7 us  [fused(): pl.pallas_call(functools.partial(network_kernel, regions, shares, slots,...]
where the time goes in v3:
time: 20.9 us; the launch traced here: 20.7 us
  Pallas kernels  19.7 us (94%)
  local copies, waits for them, and re-layouts  0.97 us (5%)
    pallas_call x1, Pallas kernels, fused(): pl.pallas_call(functools.partial(network_kernel, regions, shares, slots,...  19.7 us
    unnamed x1, local copies, waits for them, and re-layouts  0.97 us

profile of v3, /device:TPU:0, one launch (start us, length us, event | category | flops | bytes accessed | tf_op | source)
XLA Modules:
  0.0 20.7 jit_solution(7296791183227757085)
XLA Ops:
  0.0 19.7 %shard_map.64 = f32[8,128,256]{2,1,0:T(8,128)S(1)} custom-call(f32[8,128,256]{2,1,0:T(8,128)} %density_hbm.1, f32[128,256]{1,0:T(8,128)} %anchor_hbm.1, s32[4,128]{1,0:T(4,128)} %bitcast.2, s32[4,128]{1,0:T(4,128)} %bitcast.3, s32[3,128]{1,0:T(4,128)} %plan_hbm.1, f32[8]{0:T(128)} %levels_hbm.1), custom_call_target="tpu_custom_call" | custom-call | tf_op jit(solution)/shard_map/pallas_call | solution.py:414
  19.7 1.0 %copy.8 = f32[8,128,256]{2,1,0:T(8,128)} copy(f32[8,128,256]{2,1,0:T(8,128)S(1)} %shard_map.64) | data formatting | bytes 2097152
